TPU v7x, 1024 devices: a whole 4x4x32 slice. The times are simulated.
1024 devices in a mesh: tile: 128 (over x, z_hi, y, core), bin: 8 (over z_lo).
Axes of the slice: x: 4, y: 4, z: 32 (z_hi: 4, z_lo: 8; z = z_hi * 8 + z_lo), core: 2. Of those that a mesh axis runs over, the one named last changes fastest.
Arguments:
- dust_density: float32 [128, 1024, 512], P('bin', 'tile'), may hold values from 0.05 to 2
- dust_vr: float32 [128, 1024, 512], P('bin', 'tile'), may hold values from -1 to 1
- dust_va: float32 [128, 1024, 512], P('bin', 'tile'), may hold values from -1 to 1
- gas_density: float32 [1024, 512], P('tile'), may hold values from 0.5 to 2
- gas_vr: float32 [1024, 512], P('tile'), may hold values from -1 to 1
- gas_va: float32 [1024, 512], P('tile'), may hold values from -1 to 1
- stop_time: float32 [128], P('bin'), may hold values from 0.05 to 20
- gain_coef: bfloat16 [128, 128, 128], P('bin'), may hold values from -0.046875 to 0.046875
Outputs:
- density_out: float32 [128, 1024, 512], P('bin', 'tile')
- vr_out: float32 [128, 1024, 512], P('bin', 'tile')
- va_out: float32 [128, 1024, 512], P('bin', 'tile')
- gas_vr_out: float32 [1024, 512], P('tile')
- gas_va_out: float32 [1024, 512], P('tile')
All inputs are finite; a program needn't handle non-finite values.
Results may differ from a plain program's by a relative error of at most 0.0017.
Values may be sent and summed in bfloat16 or wider, within the bound.
A program may use at most 32 MiB of HBM per device.

v0:
```python
import jax
import jax.numpy as jnp
from jax import lax
from jax.sharding import PartitionSpec as P

COURANT = 0.2
COAGULATION = 0.5


def padded_2(shard, sides, width):
    for axis, dim in sides:
        count, length = (lax.axis_size(axis), shard.shape[dim])
        up = [(i, (i + 1) % count) for i in range(count - 1)]
        down = [(j, i) for i, j in up]
        last = lax.slice_in_dim(shard, length - width, length, axis=dim)
        initial = lax.slice_in_dim(shard, 0, width, axis=dim)
        before = lax.ppermute(last, axis, up)
        after = lax.ppermute(initial, axis, down)
        shard = jnp.concatenate([before, shard, after], axis=dim)
    return shard


def minmod(first, second):
    smaller = jnp.sign(first) * jnp.minimum(jnp.abs(first), jnp.abs(second))
    return jnp.where(first * second > 0, smaller, jnp.zeros_like(first))


def faces_div(values, speeds, along):
    length = values.shape[along]

    def part(array, lower, upper_cut):
        return lax.slice_in_dim(array, lower, length - upper_cut, axis=along)

    slope = minmod(part(values, 1, 1) - part(values, 0, 2), part(values, 2, 0) - part(values, 1, 1))
    centre = part(values, 1, 1)
    centre_speed = part(speeds, 1, 1)
    inner_len = length - 2

    def sub(array, lower, upper_cut):
        return lax.slice_in_dim(array, lower, inner_len - upper_cut, axis=along)

    speed = 0.5 * (sub(centre_speed, 0, 1) + sub(centre_speed, 1, 0))
    left = sub(centre, 0, 1) + 0.5 * (1.0 - speed * COURANT) * sub(slope, 0, 1)
    right = sub(centre, 1, 0) - 0.5 * (1.0 + speed * COURANT) * sub(slope, 1, 0)
    flux = jnp.maximum(speed, 0.0) * left + jnp.minimum(speed, 0.0) * right
    face_count = inner_len - 1
    return lax.slice_in_dim(flux, 1, face_count, axis=along) - lax.slice_in_dim(
        flux, 0, face_count - 1, axis=along
    )


def wrap_azimuth(field):
    return jnp.concatenate([field[..., -2:], field, field[..., :2]], axis=-1)


def coef_gain(coef_piece, densities):
    piece_bins, bin_total, _ = coef_piece.shape
    inner = jnp.dot(
        coef_piece.reshape(piece_bins * bin_total, bin_total),
        densities,
        preferred_element_type=jnp.float32,
    )
    inner = inner.reshape(piece_bins, bin_total, densities.shape[1])
    return jnp.sum(inner * densities.astype(jnp.float32)[None], axis=1)


def blocked_gain(coef_local, all_bins):
    cell_count = all_bins.shape[1]
    block_len = min(512, cell_count)
    block_total = cell_count // block_len
    result = jnp.zeros((coef_local.shape[0], cell_count), jnp.float32)

    def one_block(step_index, current):
        offset = step_index * block_len
        columns = lax.dynamic_slice_in_dim(all_bins, offset, block_len, 1)
        return lax.dynamic_update_slice_in_dim(current, coef_gain(coef_local, columns), offset, 1)

    return lax.fori_loop(0, block_total, one_block, result)


def body(dust_density, dust_vr, dust_va, gas_density, gas_vr, gas_va, stop_time, gain_coef):
    bins_here, row_count, cells_cycle = dust_density.shape
    stacked = jnp.stack([dust_density, dust_vr])
    padded = padded_2(stacked, (("tile", 2),), 2)
    padded_rho = padded[0]
    padded_speed = padded[1]
    radial_div = faces_div(padded_rho, padded_speed, 1)
    azimuth_div = faces_div(wrap_azimuth(dust_density), wrap_azimuth(dust_va), 2)
    density_adv = dust_density - COURANT * (radial_div + azimuth_div)
    drag_rate = 1.0 / stop_time
    coupling = drag_rate / (1.0 + drag_rate)
    weight = density_adv * coupling[:, None, None]
    partials = (
        jnp.sum(weight * dust_vr, axis=0),
        jnp.sum(weight * dust_va, axis=0),
        jnp.sum(weight, axis=0),
    )
    sum_radial, sum_azimuth, sum_weight = lax.psum((partials[0], partials[1], partials[2]), "bin")
    denom = gas_density + sum_weight
    gas_vr_out = (gas_density * gas_vr + sum_radial) / denom
    gas_va_out = (gas_density * gas_va + sum_azimuth) / denom
    rate_col = drag_rate[:, None, None]
    vr_out = (dust_vr + rate_col * gas_vr_out[None]) / (1.0 + rate_col)
    va_out = (dust_va + rate_col * gas_va_out[None]) / (1.0 + rate_col)
    density_low = density_adv.astype(jnp.bfloat16).reshape(bins_here, row_count * cells_cycle)
    all_bins = lax.all_gather(density_low, "bin", axis=0, tiled=True)
    gain = blocked_gain(gain_coef, all_bins)
    density_out = density_adv + COAGULATION * gain.reshape(density_adv.shape)
    return (density_out, vr_out, va_out, gas_vr_out, gas_va_out)


def solution(mesh):
    in_specs = (
        P("bin", "tile", None),
        P("bin", "tile", None),
        P("bin", "tile", None),
        P("tile", None),
        P("tile", None),
        P("tile", None),
        P("bin"),
        P("bin", None, None),
    )
    out_specs = (
        P("bin", "tile", None),
        P("bin", "tile", None),
        P("bin", "tile", None),
        P("tile", None),
        P("tile", None),
    )
    return jax.shard_map(body, mesh=mesh, in_specs=in_specs, out_specs=out_specs, check_vma=False)
```

profile of v0, /device:TPU:6, one launch (start us, length us, event | category | flops | bytes accessed | tf_op | source)
XLA Modules:
  0.0 200.0 jit_solution(13800255535583822835)
XLA Ops:
  7.2 0.0 all-gather.2.cloned.1.call-start
  7.3 1.4 pad_maximum_fusion.8
  8.6 25.2 %collective-permute-start.1 = (f32[2,16,2,512]{3,2,1,0:T(2,128)S(1)}, f32[2,16,2,512]{3,2,1,0:T(2,128)S(1)}, u32[]{:S(2)}, u32[]{:S(2)}) collective-permute-start(f32[2,16,2,512]{3,2,1,0:T(2,128)S(1)} %get-tuple-element.109), channel_id=1, source_target_pairs={{8,0},{16,8},{24,16},{32,24},{40,32},{48,40},{56,48},{64,56},{72,6... | collective-permute-start | bytes 393224 | tf_op jit(solution)/shard_map/ppermute | solution.py:18
  33.8 1.9 collective-permute-start
  35.7 1.0 fusion.20
  36.7 1.0 fusion.19
  37.6 1.5 multiply_select_fusion.1
  39.2 0.4 fusion.8
  39.6 6.7 %collective-permute-done.1 = f32[2,16,2,512]{3,2,1,0:T(2,128)S(1)} collective-permute-done((f32[2,16,2,512]{3,2,1,0:T(2,128)S(1)}, f32[2,16,2,512]{3,2,1,0:T(2,128)S(1)}, u32[]{:S(2)}, u32[]{:S(2)}) %collective-permute-start.1) | collective-permute-done | bytes 131104 | tf_op jit(solution)/shard_map/ppermute | solution.py:18
  46.3 13.2 %collective-permute-done = f32[2,16,2,512]{3,2,1,0:T(2,128)S(1)} collective-permute-done((f32[2,16,2,512]{3,2,1,0:T(2,128)S(1)}, f32[2,16,2,512]{3,2,1,0:T(2,128)S(1)}, u32[]{:S(2)}, u32[]{:S(2)}) %collective-permute-start) | collective-permute-done | bytes 131104 | tf_op jit(solution)/shard_map/ppermute | solution.py:17
  59.4 0.2 pad_maximum_fusion
  59.6 0.1 slice_bitcast_fusion.1
  59.7 0.3 multiply_select_fusion
  60.1 0.4 fusion.2
  60.6 0.2 multiply_reduce_fusion.1
  60.8 0.7 copy.19
  61.6 52.7 %all-reduce = (f32[8,512]{1,0:T(8,128)S(1)}, f32[8,512]{1,0:T(8,128)S(1)}, f32[8,512]{1,0:T(8,128)S(1)}) all-reduce(f32[8,512]{1,0:T(8,128)S(1)} %get-tuple-element.91, f32[8,512]{1,0:T(8,128)S(1)} %get-tuple-element.90, f32[8,512]{1,0:T(8,128)S(1)} %get-tuple-element.89), channel_id=1, replica_groups=mesh['tile'=128,'bin'=8] {'bin'}, use_global_device_ids=true, to_apply=%region_4.5 | all-reduce | flops 12288 | bytes 98304 | tf_op jit(solution)/shard_map/psum | solution.py:98
  114.4 1.0 add_divide_fusion
  115.4 8.4 %all-gather.2.cloned.1.call-done = bf16[128,4096]{1,0:T(8,128)(2,1)} async-done(((bf16[16,4096]{1,0:T(8,128)(2,1)}), bf16[128,4096]{1,0:T(8,128)(2,1)}) %all-gather.2.cloned.1.call-update) | async-done | bytes 1048592 | tf_op jit(solution)/shard_map/all_gather | solution.py:106
  123.8 0.1 broadcast_in_dim.4
  124.0 64.7 %while.13 = (s32[]{:T(128)}, f32[16,4096]{0,1:T(8,128)S(1)}, bf16[128,4096]{1,0:T(8,128)(2,1)}, bf16[16,128,128]{2,1,0:T(8,128)(2,1)S(1)}, s32[]{:T(128)}, /*index=5*/s32[]{:T(128)}, s32[]{:T(128)}, s32[]{:T(128)}) while((s32[]{:T(128)}, f32[16,4096]{0,1:T(8,128)S(1)}, bf16[128,4096]{1,0:T(8,128)(2,1)}, bf16[16,128,128]{2,1,0:T(8,128)(2,1)S(1)}, ...), condition=%wide.region_2.3_spmd, body=%wide.region_0.2_spmd.sunk | while | flops 270589952 | bytes 19169428 | solution.py:78
  124.0 0.9 constant_dynamic-slice_fusion.2
  124.9 0.7 convolution_bitcast_fusion.2
  125.6 2.9 %copy.22 = f32[64,8,16,128]{3,2,1,0:T(8,128)} copy(f32[64,8,16,128]{3,1,2,0:T(8,128)S(1)} %convolution_bitcast_fusion.2) | data formatting | bytes 8388608 | tf_op jit(solution)/shard_map/while
  128.5 0.1 copy.23
  128.7 3.4 %multiply_reduce_fusion.5 = f32[16,512]{0,1:T(8,128)S(1)} fusion(f32[16,128,512]{1,0,2:T(8,128)} %bitcast.28, f32[128,512]{0,1:T(8,128)S(1)} %convert_element_type.12), kind=kLoop, calls=%fused_computation.clone.1 | loop fusion | flops 2088960 | bytes 4489216 | tf_op jit(solution)/shard_map/while/body/eval_jaxpr/reduce_sum | solution.py:64
  132.1 0.9 constant_dynamic-slice_fusion.2
  133.0 0.7 convolution_bitcast_fusion.2
  133.7 2.9 %copy.22 = f32[64,8,16,128]{3,2,1,0:T(8,128)} copy(f32[64,8,16,128]{3,1,2,0:T(8,128)S(1)} %convolution_bitcast_fusion.2) | data formatting | bytes 8388608 | tf_op jit(solution)/shard_map/while
  136.6 0.1 copy.23
  136.8 3.4 %multiply_reduce_fusion.5 = f32[16,512]{0,1:T(8,128)S(1)} fusion(f32[16,128,512]{1,0,2:T(8,128)} %bitcast.28, f32[128,512]{0,1:T(8,128)S(1)} %convert_element_type.12), kind=kLoop, calls=%fused_computation.clone.1 | loop fusion | flops 2088960 | bytes 4489216 | tf_op jit(solution)/shard_map/while/body/eval_jaxpr/reduce_sum | solution.py:64
  140.2 0.9 constant_dynamic-slice_fusion.2
  141.1 0.7 convolution_bitcast_fusion.2
  141.8 2.9 %copy.22 = f32[64,8,16,128]{3,2,1,0:T(8,128)} copy(f32[64,8,16,128]{3,1,2,0:T(8,128)S(1)} %convolution_bitcast_fusion.2) | data formatting | bytes 8388608 | tf_op jit(solution)/shard_map/while
  144.7 0.1 copy.23
  144.8 3.4 %multiply_reduce_fusion.5 = f32[16,512]{0,1:T(8,128)S(1)} fusion(f32[16,128,512]{1,0,2:T(8,128)} %bitcast.28, f32[128,512]{0,1:T(8,128)S(1)} %convert_element_type.12), kind=kLoop, calls=%fused_computation.clone.1 | loop fusion | flops 2088960 | bytes 4489216 | tf_op jit(solution)/shard_map/while/body/eval_jaxpr/reduce_sum | solution.py:64
  148.3 0.9 constant_dynamic-slice_fusion.2
  149.2 0.7 convolution_bitcast_fusion.2
  149.9 2.9 %copy.22 = f32[64,8,16,128]{3,2,1,0:T(8,128)} copy(f32[64,8,16,128]{3,1,2,0:T(8,128)S(1)} %convolution_bitcast_fusion.2) | data formatting | bytes 8388608 | tf_op jit(solution)/shard_map/while
  152.8 0.1 copy.23
  152.9 3.4 %multiply_reduce_fusion.5 = f32[16,512]{0,1:T(8,128)S(1)} fusion(f32[16,128,512]{1,0,2:T(8,128)} %bitcast.28, f32[128,512]{0,1:T(8,128)S(1)} %convert_element_type.12), kind=kLoop, calls=%fused_computation.clone.1 | loop fusion | flops 2088960 | bytes 4489216 | tf_op jit(solution)/shard_map/while/body/eval_jaxpr/reduce_sum | solution.py:64
  156.4 0.9 constant_dynamic-slice_fusion.2
  157.3 0.7 convolution_bitcast_fusion.2
  158.0 2.9 %copy.22 = f32[64,8,16,128]{3,2,1,0:T(8,128)} copy(f32[64,8,16,128]{3,1,2,0:T(8,128)S(1)} %convolution_bitcast_fusion.2) | data formatting | bytes 8388608 | tf_op jit(solution)/shard_map/while
  160.9 0.1 copy.23
  161.0 3.4 %multiply_reduce_fusion.5 = f32[16,512]{0,1:T(8,128)S(1)} fusion(f32[16,128,512]{1,0,2:T(8,128)} %bitcast.28, f32[128,512]{0,1:T(8,128)S(1)} %convert_element_type.12), kind=kLoop, calls=%fused_computation.clone.1 | loop fusion | flops 2088960 | bytes 4489216 | tf_op jit(solution)/shard_map/while/body/eval_jaxpr/reduce_sum | solution.py:64
  164.4 0.9 constant_dynamic-slice_fusion.2
  165.4 0.7 convolution_bitcast_fusion.2
  166.1 2.9 %copy.22 = f32[64,8,16,128]{3,2,1,0:T(8,128)} copy(f32[64,8,16,128]{3,1,2,0:T(8,128)S(1)} %convolution_bitcast_fusion.2) | data formatting | bytes 8388608 | tf_op jit(solution)/shard_map/while
  169.0 0.1 copy.23
  169.1 3.4 %multiply_reduce_fusion.5 = f32[16,512]{0,1:T(8,128)S(1)} fusion(f32[16,128,512]{1,0,2:T(8,128)} %bitcast.28, f32[128,512]{0,1:T(8,128)S(1)} %convert_element_type.12), kind=kLoop, calls=%fused_computation.clone.1 | loop fusion | flops 2088960 | bytes 4489216 | tf_op jit(solution)/shard_map/while/body/eval_jaxpr/reduce_sum | solution.py:64
  172.5 0.9 constant_dynamic-slice_fusion.2
  173.5 0.7 convolution_bitcast_fusion.2
  174.2 2.9 %copy.22 = f32[64,8,16,128]{3,2,1,0:T(8,128)} copy(f32[64,8,16,128]{3,1,2,0:T(8,128)S(1)} %convolution_bitcast_fusion.2) | data formatting | bytes 8388608 | tf_op jit(solution)/shard_map/while
  177.1 0.1 copy.23
  177.2 3.4 %multiply_reduce_fusion.5 = f32[16,512]{0,1:T(8,128)S(1)} fusion(f32[16,128,512]{1,0,2:T(8,128)} %bitcast.28, f32[128,512]{0,1:T(8,128)S(1)} %convert_element_type.12), kind=kLoop, calls=%fused_computation.clone.1 | loop fusion | flops 2088960 | bytes 4489216 | tf_op jit(solution)/shard_map/while/body/eval_jaxpr/reduce_sum | solution.py:64
  180.6 0.9 constant_dynamic-slice_fusion.2
  181.6 0.7 convolution_bitcast_fusion.2
  182.3 2.9 %copy.22 = f32[64,8,16,128]{3,2,1,0:T(8,128)} copy(f32[64,8,16,128]{3,1,2,0:T(8,128)S(1)} %convolution_bitcast_fusion.2) | data formatting | bytes 8388608 | tf_op jit(solution)/shard_map/while
  185.2 0.1 copy.23
  185.3 3.4 %multiply_reduce_fusion.5 = f32[16,512]{0,1:T(8,128)S(1)} fusion(f32[16,128,512]{1,0,2:T(8,128)} %bitcast.28, f32[128,512]{0,1:T(8,128)S(1)} %convert_element_type.12), kind=kLoop, calls=%fused_computation.clone.1 | loop fusion | flops 2088960 | bytes 4489216 | tf_op jit(solution)/shard_map/while/body/eval_jaxpr/reduce_sum | solution.py:64
  188.7 1.5 broadcast_multiply_fusion
  190.2 2.2 %copy.16 = f32[16,8,512]{2,1,0:T(8,128)S(1)} copy(f32[16,8,512]{0,2,1:T(8,128)} %bitcast.30) | data formatting | bytes 524288 | tf_op jit(solution)/shard_map/mul | solution.py:108
  192.4 0.7 add.90
  (41 shorter events, 0.5 us)
Async XLA Ops:
  7.2 52.3 %copy-start.2 = (f32[16,8,512]{2,1,0:T(8,128)S(1)}, f32[16,8,512]{2,1,0:T(8,128)}, u32[]{:S(2)}) copy-start(f32[16,8,512]{2,1,0:T(8,128)} %param.11) | copy-start | bytes 786436
  7.2 32.0 %copy-start.1 = (f32[16,8,512]{2,1,0:T(8,128)S(1)}, f32[16,8,512]{2,1,0:T(8,128)}, u32[]{:S(2)}) copy-start(f32[16,8,512]{2,1,0:T(8,128)} %param.10) | copy-start | bytes 786436
  7.2 32.0 %copy-start.3 = (f32[16,8,512]{2,1,0:T(8,128)S(1)}, f32[16,8,512]{2,1,0:T(8,128)}, u32[]{:S(2)}) copy-start(f32[16,8,512]{2,1,0:T(8,128)} %param.12) | copy-start | bytes 786436
  7.2 32.3 %copy-start.9 = (f32[16]{0:T(128)S(1)}, f32[16]{0:T(128)}, u32[]{:S(2)}) copy-start(f32[16]{0:T(128)} %param.16) | copy-start | bytes 196
  7.2 116.6 %all-gather.2.cloned.1.call-start = ((), (), s32[]{:S(2)}) async-start(), calls=%async_computation | async-start | bytes 1179648 | tf_op jit(solution)/shard_map/all_gather | solution.py:106
  8.6 37.7 %collective-permute-start.1 = (f32[2,16,2,512]{3,2,1,0:T(2,128)S(1)}, f32[2,16,2,512]{3,2,1,0:T(2,128)S(1)}, u32[]{:S(2)}, u32[]{:S(2)}) collective-permute-start(f32[2,16,2,512]{3,2,1,0:T(2,128)S(1)} %get-tuple-element.109), channel_id=1, source_target_pairs={{8,0},{16,8},{24,16},{32,24},{40,32},{48,40},{56,48},{64,56},{72,6... | collective-permute-start | bytes 393224 | tf_op jit(solution)/shard_map/ppermute | solution.py:18
  33.8 25.7 %collective-permute-start = (f32[2,16,2,512]{3,2,1,0:T(2,128)S(1)}, f32[2,16,2,512]{3,2,1,0:T(2,128)S(1)}, u32[]{:S(2)}, u32[]{:S(2)}) collective-permute-start(f32[2,16,2,512]{3,2,1,0:T(2,128)S(1)} %get-tuple-element.108), channel_id=1, source_target_pairs={{0,8},{8,16},{16,24},{24,32},{32,40},{40,48},{48,56},{56,64},{64,7... | collective-permute-start | bytes 393224 | tf_op jit(solution)/shard_map/ppermute | solution.py:17
  60.6 53.7 %copy-start.6 = (f32[8,512]{1,0:T(8,128)S(1)}, f32[8,512]{1,0:T(8,128)}, u32[]{:S(2)}) copy-start(f32[8,512]{1,0:T(8,128)} %param.13) | copy-start | bytes 49156
  60.6 53.7 %copy-start.7 = (f32[8,512]{1,0:T(8,128)S(1)}, f32[8,512]{1,0:T(8,128)}, u32[]{:S(2)}) copy-start(f32[8,512]{1,0:T(8,128)} %param.15) | copy-start | bytes 49156
  60.6 53.7 %copy-start.8 = (f32[8,512]{1,0:T(8,128)S(1)}, f32[8,512]{1,0:T(8,128)}, u32[]{:S(2)}) copy-start(f32[8,512]{1,0:T(8,128)} %param.14) | copy-start | bytes 49156
  60.8 63.2 %copy-start = (bf16[16,128,128]{2,1,0:T(8,128)(2,1)S(1)}, bf16[16,128,128]{2,1,0:T(8,128)(2,1)}, u32[]{:S(2)}) copy-start(bf16[16,128,128]{2,1,0:T(8,128)(2,1)} %param.17) | copy-start | bytes 1572868
  114.3 9.6 %copy-start.4 = (f32[8,512]{1,0:T(8,128)}, f32[8,512]{1,0:T(8,128)S(1)}, u32[]{:S(2)}) copy-start(f32[8,512]{1,0:T(8,128)S(1)} %get-tuple-element.114) | copy-start | bytes 49156
  114.4 9.6 %copy-start.5 = (f32[8,512]{1,0:T(8,128)}, f32[8,512]{1,0:T(8,128)S(1)}, u32[]{:S(2)}) copy-start(f32[8,512]{1,0:T(8,128)S(1)} %get-tuple-element.115) | copy-start | bytes 49156
Sparse Core Ops, SparseCore 0:
  61.7 62.0 all-gather.1
where the time goes:
time: 201 us; the launch traced here: 200 us
  blocking collectives  52.7 us (26%)
  local copies, waits for them, and re-layouts  36.5 us (18%)
  other arithmetic  34.7 us (17%)
  waiting for transfers between devices  28.3 us (14%)
  starting transfers between devices  27.1 us (13%)
  between operations  14.3 us (7%)
  matrix products  5.88 us (3%)
    psum x1, blocking collectives, body(): lax.psum((partials[0], partials[1], partials[2]), 'bin')  52.7 us
    reduce_sum x8, other arithmetic, coef_gain(): return jnp.sum(inner * densities.astype(jnp.float32)[None], axis=1)  26.9 us
    ppermute x1, starting transfers between devices, padded_2(): after = lax.ppermute(initial, axis, down)  25.2 us
    while x8, local copies, waits for them, and re-layouts  22.9 us
    ppermute x1, waiting for transfers between devices, padded_2(): before = lax.ppermute(last, axis, up)  13.2 us
    all_gather x1, waiting for transfers between devices, body(): all_bins = lax.all_gather(density_low, 'bin', axis=0, tiled=True)  8.44 us
    dynamic_slice x16, local copies, waits for them, and re-layouts, one_block(): columns = lax.dynamic_slice_in_dim(all_bins, offset, block_len, 1)  8.28 us
    ppermute x1, waiting for transfers between devices, padded_2(): after = lax.ppermute(initial, axis, down)  6.72 us
  transfers between devices with their start and end apart: 3, of which 3 were waited for; matrix products, arithmetic and copies ran while one was open for 2% of the time, Pallas kernels for 0%

commit v1 on v0

v1 whole, which is shorter than its diff:
```python
import functools

import jax
import jax.numpy as jnp
from jax import lax
from jax.experimental import pallas as pl
from jax.experimental.pallas import tpu as pltpu
from jax.sharding import PartitionSpec as P

COURANT = 0.2
COAGULATION = 0.5
TILE_SPLIT = {128: (4, 4, 4, 2)}
QUAD = 4
ROWS = 8
LANES = 128
CHUNKS = 4
VMEM_BYTES = 40 * 2**20
ROW_ORDER = (2, 3, 4, 5, 0, 1, 6, 7)
MESH = pl.DeviceIdType.MESH
F32 = jnp.float32
BF16 = jnp.bfloat16


def minmod(a, b):
    return jnp.maximum(jnp.minimum(a, b), 0.0) + jnp.minimum(jnp.maximum(a, b), 0.0)


def face_flux(q, q_next, s, s_next, v, v_next):
    u = 0.5 * (v + v_next)
    forward = u > 0
    reach = 0.5 - 0.5 * COURANT * jnp.abs(u)
    return u * (jnp.where(forward, q, q_next) + reach * jnp.where(forward, s, -s_next))


def azimuth_div(q, v):
    cells = q.shape[1]

    def ahead(x):
        return pltpu.roll(x, cells - 1, 1)

    def behind(x):
        return pltpu.roll(x, 1, 1)

    q_next = ahead(q)
    step = q_next - q
    s = minmod(behind(step), step)
    flux = face_flux(q, q_next, s, ahead(s), v, ahead(v))
    return flux - behind(flux)


def kernel(
    split,
    tiles,
    rho_hbm,
    vr_hbm,
    va_hbm,
    coef_hbm,
    stop,
    gas_rho_hbm,
    gas_vr_hbm,
    gas_va_hbm,
    tiles_out,
    gas_out,
    tiles_in,
    gas_in,
    own_coef,
    mate_coef,
    q_rows,
    v_rows,
    a_rows,
    edge_send,
    edge_recv,
    adv,
    halves,
    all_bins,
    partial,
    partial_in,
    quad_sum,
    gas_rows,
    gain_send,
    gain_recv,
    load_sem,
    halo_send,
    halo_recv,
    give_send,
    item_recv,
    up_send,
    down_send,
    gain_send_sem,
    gain_recv_sem,
    coef_send,
    coef_recv,
    sum_send,
    sum_recv,
):
    xs, hs, ys, cores = split
    bins, cells = q_rows.shape[1:]
    half = cells // 2
    lane_tiles = cells // LANES
    t = lax.axis_index("tile")
    z = lax.axis_index("bin")
    core = t % cores
    y = (t // cores) % ys
    z_hi = (t // (cores * ys)) % hs
    x = t // (cores * ys * hs)
    w = z % QUAD
    quad = z // QUAD
    mate = (z + QUAD) % (2 * QUAD)
    own_base = quad * QUAD
    other_base = QUAD - own_base

    def tile_at(x_, y_, core_):
        return ((x_ * hs + z_hi) * ys + y_) * cores + core_

    def quad_at(i):
        return own_base + (w + i) % QUAD

    def lane_tile(l):
        return pl.ds(l * LANES, LANES)

    loads = [
        [
            pltpu.make_async_copy(src.at[:, lane_tile(l)], tiles_in.at[i, l], load_sem.at[i, l])
            for l in range(lane_tiles)
        ]
        for i, src in enumerate((rho_hbm, vr_hbm, va_hbm))
    ]
    load_coef = pltpu.make_async_copy(coef_hbm, own_coef, load_sem.at[3, 0])
    load_gas = [
        pltpu.make_async_copy(src, gas_in.at[i], load_sem.at[3, 1 + i])
        for i, src in enumerate((gas_rho_hbm, gas_vr_hbm, gas_va_hbm))
    ]
    for group in loads:
        for load in group:
            load.start()
    load_coef.start()
    for load in load_gas:
        load.start()

    barrier = pltpu.get_barrier_semaphore()
    peers = [(t, mate)] + [(t, quad_at(i)) for i in range(1, QUAD)]
    peers += [(tile_at(x, (y + i) % ys, core), z) for i in range(1, ys)]
    peers += [(tile_at((x + i) % xs, y, core), z) for i in range(1, xs)]
    peers += [((t + 1) % tiles, z), ((t + tiles - 1) % tiles, z)]
    for peer in peers:
        pl.semaphore_signal(barrier, inc=1, device_id=peer, device_id_type=MESH)

    has_prev = t > 0
    has_next = t < tiles - 1
    prev_dev = (jnp.maximum(t - 1, 0), z)
    next_dev = (jnp.minimum(t + 1, tiles - 1), z)

    stop_bin = lax.broadcasted_iota(jnp.int32, (bins, 1), 0)
    stop_col = jnp.zeros((bins, 1), F32)
    for b in range(bins):
        stop_col = jnp.where(stop_bin == b, stop[b], stop_col)
    couple = 1.0 / (1.0 + stop_col)
    keep = stop_col * couple

    partial[...] = jnp.zeros_like(partial)
    for group, rows, first in zip(loads, (q_rows, v_rows, a_rows), (2, 1, 0)):
        i = 2 - first
        for l, load in enumerate(group):
            load.wait()
            for r in range(ROWS):
                rows[first + r, :, lane_tile(l)] = tiles_in[i, l, pl.ds(r, bins, stride=ROWS), :]

    def put(i, r, value):
        for l in range(lane_tiles):
            tiles_out[i, l, pl.ds(r, bins, stride=ROWS), :] = value[:, l * LANES : (l + 1) * LANES]

    for i, (first, speed) in enumerate(((ROWS, ROWS), (2, 1))):
        edge_send[i, 0:2] = q_rows[first : first + 2].astype(BF16)
        edge_send[i, 2] = v_rows[speed].astype(BF16)

    pl.semaphore_wait(barrier, len(peers))

    def halo(i, device):
        return pltpu.make_async_remote_copy(
            src_ref=edge_send.at[i],
            dst_ref=edge_recv.at[i],
            send_sem=halo_send.at[i],
            recv_sem=halo_recv.at[i],
            device_id=device,
            device_id_type=MESH,
        )

    to_next, to_prev = halo(0, next_dev), halo(1, prev_dev)

    @pl.when(has_next)
    def _():
        to_next.start()

    @pl.when(has_prev)
    def _():
        to_prev.start()

    piece_rows = mate_coef.shape[3]
    piece = (core * xs + x) * ys + y

    def coef_copy(i, src, dst, device):
        return pltpu.make_async_remote_copy(
            src_ref=src,
            dst_ref=dst,
            send_sem=coef_send.at[i],
            recv_sem=coef_recv.at[i],
            device_id=device,
            device_id_type=MESH,
        )

    coef_from_mate = coef_copy(
        0,
        coef_hbm.at[pl.ds(pl.multiple_of(piece * piece_rows, piece_rows), piece_rows)],
        mate_coef.at[core, x, y],
        (t, mate),
    )
    coef_y = [
        coef_copy(i, mate_coef.at[core, x, y], mate_coef.at[core, x, y], (tile_at(x, (y + i) % ys, core), z))
        for i in range(1, ys)
    ]
    coef_x = [
        coef_copy(3 + i, mate_coef.at[core, x], mate_coef.at[core, x], (tile_at((x + i) % xs, y, core), z))
        for i in range(1, xs)
    ]
    coef_core = [
        coef_copy(6 + i, mate_coef.at[core], mate_coef.at[core], (tile_at(x, y, (core + i) % cores), z))
        for i in range(1, cores)
    ]

    def give(c):
        return pltpu.make_async_remote_copy(
            src_ref=halves.at[c, 1 - quad],
            dst_ref=all_bins.at[c, z],
            send_sem=give_send.at[c],
            recv_sem=item_recv.at[c, z],
            device_id=(t, mate),
            device_id_type=MESH,
        )

    def taken(c):
        return pltpu.make_async_remote_copy(
            src_ref=halves.at[c, 1 - quad],
            dst_ref=all_bins.at[c, mate],
            send_sem=give_send.at[c],
            recv_sem=item_recv.at[c, mate],
            device_id=(t, mate),
            device_id_type=MESH,
        )

    def pass_on(c, d, place, up):
        return pltpu.make_async_remote_copy(
            src_ref=all_bins.at[c, d],
            dst_ref=all_bins.at[c, d],
            send_sem=(up_send if up else down_send).at[place],
            recv_sem=item_recv.at[c, d],
            device_id=(t, jnp.minimum(z + 1, 2 * QUAD - 1) if up else jnp.maximum(z - 1, 0)),
            device_id_type=MESH,
        )

    can_up = w < QUAD - 1
    can_down = w > 0

    def send_both(c, d):
        @pl.when(can_up)
        def _():
            pass_on(c, d, w, True).start()

        @pl.when(can_down)
        def _():
            pass_on(c, d, w, False).start()

    def relay(c, far):
        @pl.when(w >= far)
        def _():
            for base in (own_base, other_base):
                d = base + jnp.maximum(w - far, 0)
                pass_on(c, d, jnp.maximum(w - far, 0), True).wait_recv()
                if far < QUAD - 1:

                    @pl.when(can_up)
                    def _():
                        pass_on(c, d, jnp.maximum(w - far, 0), True).start()

        @pl.when(w + far < QUAD)
        def _():
            for base in (own_base, other_base):
                d = base + jnp.minimum(w + far, QUAD - 1)
                pass_on(c, d, jnp.minimum(w + far, QUAD - 1), False).wait_recv()
                if far < QUAD - 1:

                    @pl.when(can_down)
                    def _():
                        pass_on(c, d, jnp.minimum(w + far, QUAD - 1), False).start()

    def take_mates(c):
        taken(c).wait_recv()
        send_both(c, mate)

    def slope(i):
        return minmod(q_rows[i] - q_rows[i - 1], q_rows[i + 1] - q_rows[i])

    def radial_flux(r):
        return face_flux(
            q_rows[r + 1], q_rows[r + 2], slope(r + 1), slope(r + 2), v_rows[r], v_rows[r + 1]
        )

    def advect(c):
        before = None
        for j in range(2):
            r = ROW_ORDER[2 * c + j]
            if before is None:
                before = radial_flux(r)
            after = radial_flux(r + 1)
            v_a = a_rows[r]
            q = q_rows[2 + r]
            new = q - COURANT * ((after - before) + azimuth_div(q, v_a))
            before = after
            adv[r] = new
            low = new.astype(BF16)
            halves[c, 0, j] = low[:, :half]
            halves[c, 1, j] = low[:, half:]
            weight = new * couple
            for n, term in enumerate((weight * v_rows[1 + r], weight * v_a, weight)):
                partial[r // 2, pl.ds(3 * j + n, 1), :] = jnp.sum(term, axis=0, keepdims=True)

    def launch(c):
        all_bins[c, z] = halves[c, quad]
        give(c).start()
        send_both(c, z)

    def gains(c, coef, j):
        low = all_bins[c, :, j].reshape(2 * QUAD * bins, half)
        wide = low.astype(F32).reshape(1, 2 * QUAD * bins // 8, 8, half)
        inner = jnp.dot(coef, low, preferred_element_type=F32)
        terms = inner.reshape(bins, 2 * QUAD * bins // 8, 8, half) * wide
        return jnp.sum(jnp.sum(terms, axis=1), axis=1)

    def gain_copy(c):
        return pltpu.make_async_remote_copy(
            src_ref=gain_send.at[c],
            dst_ref=gain_recv.at[c],
            send_sem=gain_send_sem.at[c],
            recv_sem=gain_recv_sem.at[c],
            device_id=(t, mate),
            device_id_type=MESH,
        )

    def mate_gains(c):
        coef = mate_coef[...].reshape(own_coef.shape)
        for j in range(2):
            gain_send[c, j] = gains(c, coef, j).astype(BF16)
        gain_copy(c).start()

    def own_gains(c):
        coef = own_coef[...]
        for j in range(2):
            r = ROW_ORDER[2 * c + j]
            lanes = pl.ds(pl.multiple_of(quad * half, half), half)
            adv[r, :, lanes] = adv[r, :, lanes] + COAGULATION * gains(c, coef, j)

    def finish(c):
        gain_copy(c).wait_recv()
        for j in range(2):
            r = ROW_ORDER[2 * c + j]
            lanes = pl.ds(pl.multiple_of((1 - quad) * half, half), half)
            adv[r, :, lanes] = adv[r, :, lanes] + COAGULATION * gain_recv[c, j].astype(F32)
            put(0, r, adv[r])

    def sum_copy(i, src, dst, device):
        return pltpu.make_async_remote_copy(
            src_ref=src,
            dst_ref=dst,
            send_sem=sum_send.at[i],
            recv_sem=sum_recv.at[i],
            device_id=device,
            device_id_type=MESH,
        )

    spread = [
        sum_copy(i, partial.at[(w + i) % QUAD], partial_in.at[i], (t, quad_at(i))) for i in range(1, QUAD)
    ]
    across = sum_copy(QUAD, quad_sum.at[0], quad_sum.at[1], (t, mate))
    shared = [
        sum_copy(QUAD + i, gas_rows.at[w], gas_rows.at[w], (t, quad_at(i))) for i in range(1, QUAD)
    ]
    shared_in = [
        sum_copy(QUAD + i, gas_rows.at[(w - i + QUAD) % QUAD], gas_rows.at[(w - i + QUAD) % QUAD], (t, quad_at(i)))
        for i in range(1, QUAD)
    ]

    def sum_across():
        total = partial[w]
        for copy in spread:
            copy.wait_recv()
        for i in range(1, QUAD):
            total = total + partial_in[i]
        quad_sum[0] = total
        across.start()

    def gas_step():
        for load in load_gas:
            load.wait()
        across.wait_recv()
        total = quad_sum[0] + quad_sum[1]
        for j in range(2):
            row = pl.ds(2 * w + j, 1)
            dense = gas_in[0, row, :]
            share = 1.0 / (dense + total[3 * j + 2 : 3 * j + 3])
            gas_rows[w, pl.ds(2 * j, 1), :] = (dense * gas_in[1, row, :] + total[3 * j : 3 * j + 1]) * share
            gas_rows[w, pl.ds(2 * j + 1, 1), :] = (dense * gas_in[2, row, :] + total[3 * j + 1 : 3 * j + 2]) * share
        for copy in shared:
            copy.start()

    def dust_speeds():
        for copy in shared_in:
            copy.wait_recv()
        for r in range(ROWS):
            u, j = r // 2, r % 2
            gas_r = gas_rows[u, pl.ds(2 * j, 1), :]
            gas_a = gas_rows[u, pl.ds(2 * j + 1, 1), :]
            gas_out[0, pl.ds(r, 1), :] = gas_r
            gas_out[1, pl.ds(r, 1), :] = gas_a
            put(1, r, v_rows[1 + r] * keep + gas_r * couple)
            put(2, r, a_rows[r] * keep + gas_a * couple)

    def halo_in():
        @pl.when(has_prev)
        def _():
            to_next.wait_recv()
            q_rows[0:2] = edge_recv[0, 0:2].astype(F32)
            v_rows[0] = edge_recv[0, 2].astype(F32)

        @pl.when(t == 0)
        def _():
            q_rows[0:2] = jnp.zeros_like(q_rows[0:2])
            v_rows[0] = jnp.zeros_like(v_rows[0])

        @pl.when(has_next)
        def _():
            to_prev.wait_recv()
            q_rows[ROWS + 2 : ROWS + 4] = edge_recv[1, 0:2].astype(F32)
            v_rows[ROWS + 1] = edge_recv[1, 2].astype(F32)

        @pl.when(t == tiles - 1)
        def _():
            q_rows[ROWS + 2 : ROWS + 4] = jnp.zeros_like(q_rows[0:2])
            v_rows[ROWS + 1] = jnp.zeros_like(v_rows[0])

    coef_from_mate.start()
    advect(0)
    launch(0)
    advect(1)
    launch(1)
    take_mates(0)
    relay(0, 1)
    take_mates(1)
    coef_from_mate.wait_recv()
    for copy in coef_y:
        copy.start()
    relay(1, 1)
    halo_in()
    advect(2)
    launch(2)
    advect(3)
    launch(3)
    for copy in spread:
        copy.start()
    relay(0, 2)
    for copy in coef_y:
        copy.wait_recv()
    for copy in coef_x:
        copy.start()
    relay(1, 2)
    take_mates(2)
    relay(2, 1)
    take_mates(3)
    relay(3, 1)
    load_coef.wait()
    relay(0, 3)
    own_gains(0)
    relay(2, 2)
    sum_across()
    for copy in coef_x:
        copy.wait_recv()
    for copy in coef_core:
        copy.start()
    relay(3, 2)
    relay(1, 3)
    own_gains(1)
    for copy in coef_core:
        copy.wait_recv()
    mate_gains(0)
    mate_gains(1)
    gas_step()
    relay(2, 3)
    mate_gains(2)
    relay(3, 3)
    mate_gains(3)
    own_gains(2)
    dust_speeds()
    own_gains(3)
    for c in range(CHUNKS):
        finish(c)

    @pl.when(has_next)
    def _():
        to_next.wait_send()

    @pl.when(has_prev)
    def _():
        to_prev.wait_send()

    for copy in [coef_from_mate, across] + coef_y + coef_x + coef_core + spread + shared:
        copy.wait_send()
    for c in range(CHUNKS):
        give(c).wait_send()
        gain_copy(c).wait_send()
    for place in range(QUAD):
        for up in (True, False):

            @pl.when((can_up if up else can_down) & (place <= w if up else place >= w))
            def _():
                pltpu.make_async_remote_copy(
                    src_ref=all_bins.at[:, pl.ds(0, 2)],
                    dst_ref=all_bins.at[:, pl.ds(0, 2)],
                    send_sem=(up_send if up else down_send).at[place],
                    recv_sem=item_recv.at[0, 0],
                    device_id=(t, mate),
                    device_id_type=MESH,
                ).wait_send()


def write_out(tiles, gas, rho_out, vr_out, va_out, gas_vr_out, gas_va_out, sem, gas_sem):
    copies = [pltpu.make_async_copy(gas.at[i], out, gas_sem.at[i]) for i, out in enumerate((gas_vr_out, gas_va_out))]
    for i, out in enumerate((rho_out, vr_out, va_out)):
        for l in range(tiles.shape[1]):
            lanes = pl.ds(l * LANES, LANES)
            copies.append(pltpu.make_async_copy(tiles.at[i, l], out.at[:, lanes], sem.at[i, l]))
    for copy in copies:
        copy.start()
    for copy in copies:
        copy.wait()


def step(split, tiles, rho, vr, va, gas_rho, gas_vr, gas_va, stop, coef):
    bins, rows, cells = rho.shape
    half = cells // 2
    flat = (bins * rows, cells)
    total_bins = coef.shape[1]
    xs, _, ys, cores = split
    coef = coef.reshape(bins * total_bins, total_bins)
    dma = pltpu.SemaphoreType.DMA
    hbm = pl.BlockSpec(memory_space=pltpu.HBM)
    vmem = pl.BlockSpec(memory_space=pltpu.VMEM)
    lane_tiles = cells // LANES
    out_shape = [jax.ShapeDtypeStruct(flat, F32)] * 3 + [jax.ShapeDtypeStruct((rows, cells), F32)] * 2
    results = pl.pallas_call(
        functools.partial(kernel, split, tiles),
        out_shape=[
            jax.ShapeDtypeStruct((3, lane_tiles, flat[0], LANES), F32),
            jax.ShapeDtypeStruct((2, rows, cells), F32),
        ],
        in_specs=[hbm] * 4 + [pl.BlockSpec(memory_space=pltpu.SMEM)] + [hbm] * 3,
        out_specs=[vmem] * 2,
        scratch_shapes=[
            pltpu.VMEM((3, lane_tiles, flat[0], LANES), F32),
            pltpu.VMEM((3, rows, cells), F32),
            pltpu.VMEM(coef.shape, BF16),
            pltpu.VMEM((cores, xs, ys, coef.shape[0] // (cores * xs * ys), total_bins), BF16),
            pltpu.VMEM((rows + 4, bins, cells), F32),
            pltpu.VMEM((rows + 2, bins, cells), F32),
            pltpu.VMEM((rows, bins, cells), F32),
            pltpu.VMEM((2, 3, bins, cells), BF16),
            pltpu.VMEM((2, 3, bins, cells), BF16),
            pltpu.VMEM((rows, bins, cells), F32),
            pltpu.VMEM((CHUNKS, 2, 2, bins, half), BF16),
            pltpu.VMEM((CHUNKS, 2 * QUAD, 2, bins, half), BF16),
            pltpu.VMEM((QUAD, 8, cells), F32),
            pltpu.VMEM((QUAD, 8, cells), F32),
            pltpu.VMEM((2, 8, cells), F32),
            pltpu.VMEM((QUAD, 4, cells), F32),
            pltpu.VMEM((CHUNKS, 2, bins, half), BF16),
            pltpu.VMEM((CHUNKS, 2, bins, half), BF16),
            dma((4, lane_tiles)),
            dma((2,)),
            dma((2,)),
            dma((CHUNKS,)),
            dma((CHUNKS, 2 * QUAD)),
            dma((QUAD,)),
            dma((QUAD,)),
            dma((CHUNKS,)),
            dma((CHUNKS,)),
            dma((8,)),
            dma((8,)),
            dma((2 * QUAD,)),
            dma((2 * QUAD,)),
        ],
        compiler_params=pltpu.CompilerParams(
            collective_id=0, has_side_effects=True, vmem_limit_bytes=VMEM_BYTES
        ),
    )(
        *(pltpu.with_memory_space_constraint(x, pltpu.HBM) for x in (rho.reshape(flat), vr.reshape(flat), va.reshape(flat), coef)),
        stop,
        *(pltpu.with_memory_space_constraint(x, pltpu.HBM) for x in (gas_rho, gas_vr, gas_va)),
    )
    outs = pl.pallas_call(
        write_out,
        out_shape=out_shape,
        in_specs=[vmem] * 2,
        out_specs=[hbm] * 5,
        scratch_shapes=[dma((3, lane_tiles)), dma((2,))],
        compiler_params=pltpu.CompilerParams(vmem_limit_bytes=VMEM_BYTES),
    )(*results)
    return tuple(out.reshape(rho.shape) for out in outs[:3]) + tuple(outs[3:])


def solution(mesh):
    tiles = mesh.shape["tile"]
    grid = P("bin", "tile", None)
    gas = P("tile", None)
    return jax.shard_map(
        functools.partial(step, TILE_SPLIT[tiles], tiles),
        mesh=mesh,
        in_specs=(grid, grid, grid, gas, gas, gas, P("bin"), P("bin", None, None)),
        out_specs=(grid, grid, grid, gas, gas),
        check_vma=False,
    )
```

time: 201 us -> 67.2 us (0.33)
  Pallas kernels: 0 us -> 65.8 us
  blocking collectives: 52.7 us -> 0 us
  local copies, waits for them, and re-layouts: 36.5 us -> 0.65 us
  other arithmetic: 34.7 us -> 0 us
  waiting for transfers between devices: 28.3 us -> 0 us
  starting transfers between devices: 27.1 us -> 0 us
  between operations: 14.3 us -> 0.65 us
  matrix products: 5.88 us -> 0 us
    pallas_call x0 -> x2, Pallas kernels: none -> 65.8 us  [the longest x1 64.8 us: step(): pl.pallas_call(functools.partial(kernel, split, tiles), out_shape=[jax.Sh...]
    psum x1 -> x0, blocking collectives: 52.7 us -> none  [body(): lax.psum((partials[0], partials[1], partials[2]), 'bin')]
    ppermute x2 -> x0, starting transfers between devices: 27.1 us -> none  [the longest x1 25.2 us: padded_2(): after = lax.ppermute(initial, axis, down)]
    reduce_sum x9 -> x0, other arithmetic: 27 us -> none  [the longest x8 26.9 us: coef_gain(): return jnp.sum(inner * densities.astype(jnp.float32)[None], axis=1)]
    while x8 -> x0, local copies, waits for them, and re-layouts: 22.9 us -> none
    ppermute x2 -> x0, waiting for transfers between devices: 19.9 us -> none  [the longest x1 13.2 us: padded_2(): before = lax.ppermute(last, axis, up)]
    all_gather x1 -> x0, waiting for transfers between devices: 8.44 us -> none  [body(): all_bins = lax.all_gather(density_low, 'bin', axis=0, tiled=True)]
    dynamic_slice x16 -> x0, local copies, waits for them, and re-layouts: 8.28 us -> none  [one_block(): columns = lax.dynamic_slice_in_dim(all_bins, offset, block_len, 1)]
  transfers between devices with their start and end apart: 3 -> 0, of which waited for: 3 -> 0; matrix products, arithmetic and copies ran while one was open for 2% -> 0% of each run, Pallas kernels for 0% -> 0%
where the time goes in v1:
time: 67.2 us; the launch traced here: 67.1 us
  Pallas kernels  65.8 us (98%)
    pallas_call x1, Pallas kernels, step(): pl.pallas_call(functools.partial(kernel, split, tiles), out_shape=[jax.Sh...  64.8 us

profile of v1, /device:TPU:6, one launch (start us, length us, event | category | flops | bytes accessed | tf_op | source)
XLA Modules:
  0.0 67.1 jit_solution(13631966018358660969)
XLA Ops:
  0.6 0.0 copy-start
  0.6 0.6 copy-done
  1.3 64.8 %shard_map.119 = (f32[3,4,128,128]{3,2,1,0:T(8,128)S(1)}, f32[2,8,512]{2,1,0:T(8,128)S(1)}) custom-call(f32[128,512]{1,0:T(8,128)} %bitcast.8, f32[128,512]{1,0:T(8,128)} %bitcast.9, f32[128,512]{1,0:T(8,128)} %bitcast.10, bf16[2048,128]{1,0:T(8,128)(2,1)} %bitcast.7, f32[16]{0:T(128)S(1)} %copy-done, f32[8,512]{1,0:T(8,128)} %gas_rho_hbm.1, ...), custom_call_target="tpu_custom_call" | custom-call | tf_op jit(solution)/shard_map/pallas_call | solution.py:557
  66.1 1.0 %shard_map.120 = (f32[128,512]{1,0:T(8,128)}, f32[128,512]{1,0:T(8,128)}, f32[128,512]{1,0:T(8,128)}, f32[8,512]{1,0:T(8,128)}, f32[8,512]{1,0:T(8,128)}) custom-call(f32[3,4,128,128]{3,2,1,0:T(8,128)S(1)} %get-tuple-element.12.tiles, f32[2,8,512]{2,1,0:T(8,128)S(1)} %get-tuple-element.13.gas), custom_call_target="tpu_custom_call" | custom-call | tf_op jit(solution)/shard_map/pallas_call | solution.py:606
Async XLA Ops:
  0.6 0.7 copy-start

commit v2 on v1

--- a/solution.py
+++ b/solution.py
@@ -13,7 +13,8 @@
 QUAD = 4
 ROWS = 8
 LANES = 128
-CHUNKS = 4
+CHUNKS = 2
+DEEP = ROWS // CHUNKS
 VMEM_BYTES = 40 * 2**20
 ROW_ORDER = (2, 3, 4, 5, 0, 1, 6, 7)
 MESH = pl.DeviceIdType.MESH
@@ -269,28 +270,32 @@
         def _():
             pass_on(c, d, w, False).start()
 
-    def relay(c, far):
+    def relay(c, far, base):
         @pl.when(w >= far)
         def _():
-            for base in (own_base, other_base):
-                d = base + jnp.maximum(w - far, 0)
-                pass_on(c, d, jnp.maximum(w - far, 0), True).wait_recv()
-                if far < QUAD - 1:
-
-                    @pl.when(can_up)
-                    def _():
-                        pass_on(c, d, jnp.maximum(w - far, 0), True).start()
+            place = jnp.maximum(w - far, 0)
+            pass_on(c, base + place, place, True).wait_recv()
+            if far < QUAD - 1:
+
+                @pl.when(can_up)
+                def _():
+                    pass_on(c, base + place, place, True).start()
 
         @pl.when(w + far < QUAD)
         def _():
-            for base in (own_base, other_base):
-                d = base + jnp.minimum(w + far, QUAD - 1)
-                pass_on(c, d, jnp.minimum(w + far, QUAD - 1), False).wait_recv()
-                if far < QUAD - 1:
-
-                    @pl.when(can_down)
-                    def _():
-                        pass_on(c, d, jnp.minimum(w + far, QUAD - 1), False).start()
+            place = jnp.minimum(w + far, QUAD - 1)
+            pass_on(c, base + place, place, False).wait_recv()
+            if far < QUAD - 1:
+
+                @pl.when(can_down)
+                def _():
+                    pass_on(c, base + place, place, False).start()
+
+    def own_relay(c, far):
+        relay(c, far, own_base)
+
+    def mate_relay(c, far):
+        relay(c, far, other_base)
 
     def take_mates(c):
         taken(c).wait_recv()
@@ -305,11 +310,12 @@
         )
 
     def advect(c):
-        before = None
-        for j in range(2):
-            r = ROW_ORDER[2 * c + j]
-            if before is None:
+        before, last = None, None
+        for j in range(DEEP):
+            r = ROW_ORDER[DEEP * c + j]
+            if last != r - 1:
                 before = radial_flux(r)
+            last = r
             after = radial_flux(r + 1)
             v_a = a_rows[r]
             q = q_rows[2 + r]
@@ -321,7 +327,7 @@
             halves[c, 1, j] = low[:, half:]
             weight = new * couple
             for n, term in enumerate((weight * v_rows[1 + r], weight * v_a, weight)):
-                partial[r // 2, pl.ds(3 * j + n, 1), :] = jnp.sum(term, axis=0, keepdims=True)
+                partial[r // 2, pl.ds(3 * (r % 2) + n, 1), :] = jnp.sum(term, axis=0, keepdims=True)
 
     def launch(c):
         all_bins[c, z] = halves[c, quad]
@@ -347,21 +353,21 @@
 
     def mate_gains(c):
         coef = mate_coef[...].reshape(own_coef.shape)
-        for j in range(2):
+        for j in range(DEEP):
             gain_send[c, j] = gains(c, coef, j).astype(BF16)
         gain_copy(c).start()
 
     def own_gains(c):
         coef = own_coef[...]
-        for j in range(2):
-            r = ROW_ORDER[2 * c + j]
+        for j in range(DEEP):
+            r = ROW_ORDER[DEEP * c + j]
             lanes = pl.ds(pl.multiple_of(quad * half, half), half)
             adv[r, :, lanes] = adv[r, :, lanes] + COAGULATION * gains(c, coef, j)
 
     def finish(c):
         gain_copy(c).wait_recv()
-        for j in range(2):
-            r = ROW_ORDER[2 * c + j]
+        for j in range(DEEP):
+            r = ROW_ORDER[DEEP * c + j]
             lanes = pl.ds(pl.multiple_of((1 - quad) * half, half), half)
             adv[r, :, lanes] = adv[r, :, lanes] + COAGULATION * gain_recv[c, j].astype(F32)
             put(0, r, adv[r])
@@ -446,59 +452,50 @@
             q_rows[ROWS + 2 : ROWS + 4] = jnp.zeros_like(q_rows[0:2])
             v_rows[ROWS + 1] = jnp.zeros_like(v_rows[0])
 
+    def start(copies):
+        for copy in copies:
+            copy.start()
+
+    def receive(copies):
+        for copy in copies:
+            copy.wait_recv()
+
     coef_from_mate.start()
     advect(0)
     launch(0)
+    coef_from_mate.wait_recv()
+    start(coef_y)
+    own_relay(0, 1)
+    halo_in()
     advect(1)
     launch(1)
+    start(spread)
     take_mates(0)
-    relay(0, 1)
+    own_relay(0, 2)
+    receive(coef_y)
+    start(coef_x)
+    own_relay(1, 1)
+    mate_relay(0, 1)
+    sum_across()
+    own_relay(1, 2)
     take_mates(1)
-    coef_from_mate.wait_recv()
-    for copy in coef_y:
-        copy.start()
-    relay(1, 1)
-    halo_in()
-    advect(2)
-    launch(2)
-    advect(3)
-    launch(3)
-    for copy in spread:
-        copy.start()
-    relay(0, 2)
-    for copy in coef_y:
-        copy.wait_recv()
-    for copy in coef_x:
-        copy.start()
-    relay(1, 2)
-    take_mates(2)
-    relay(2, 1)
-    take_mates(3)
-    relay(3, 1)
+    mate_relay(0, 2)
+    receive(coef_x)
+    start(coef_core)
+    mate_relay(1, 1)
+    gas_step()
     load_coef.wait()
-    relay(0, 3)
+    own_relay(0, 3)
+    mate_relay(0, 3)
+    mate_relay(1, 2)
     own_gains(0)
-    relay(2, 2)
-    sum_across()
-    for copy in coef_x:
-        copy.wait_recv()
-    for copy in coef_core:
-        copy.start()
-    relay(3, 2)
-    relay(1, 3)
+    receive(coef_core)
+    mate_gains(0)
+    own_relay(1, 3)
+    mate_relay(1, 3)
+    mate_gains(1)
+    dust_speeds()
     own_gains(1)
-    for copy in coef_core:
-        copy.wait_recv()
-    mate_gains(0)
-    mate_gains(1)
-    gas_step()
-    relay(2, 3)
-    mate_gains(2)
-    relay(3, 3)
-    mate_gains(3)
-    own_gains(2)
-    dust_speeds()
-    own_gains(3)
     for c in range(CHUNKS):
         finish(c)
 
@@ -573,14 +570,14 @@
             pltpu.VMEM((2, 3, bins, cells), BF16),
             pltpu.VMEM((2, 3, bins, cells), BF16),
             pltpu.VMEM((rows, bins, cells), F32),
-            pltpu.VMEM((CHUNKS, 2, 2, bins, half), BF16),
-            pltpu.VMEM((CHUNKS, 2 * QUAD, 2, bins, half), BF16),
+            pltpu.VMEM((CHUNKS, 2, DEEP, bins, half), BF16),
+            pltpu.VMEM((CHUNKS, 2 * QUAD, DEEP, bins, half), BF16),
             pltpu.VMEM((QUAD, 8, cells), F32),
             pltpu.VMEM((QUAD, 8, cells), F32),
             pltpu.VMEM((2, 8, cells), F32),
             pltpu.VMEM((QUAD, 4, cells), F32),
-            pltpu.VMEM((CHUNKS, 2, bins, half), BF16),
-            pltpu.VMEM((CHUNKS, 2, bins, half), BF16),
+            pltpu.VMEM((CHUNKS, DEEP, bins, half), BF16),
+            pltpu.VMEM((CHUNKS, DEEP, bins, half), BF16),
             dma((4, lane_tiles)),
             dma((2,)),
             dma((2,)),

time: 67.2 us -> 58.4 us (0.87)
  Pallas kernels: 65.8 us -> 56.9 us
    pallas_call x1, Pallas kernels: 64.8 us -> 55.9 us  [step(): pl.pallas_call(functools.partial(kernel, split, tiles), out_shape=[jax.Sh...]
where the time goes in v2:
time: 58.4 us; the launch traced here: 58.2 us
  Pallas kernels  56.9 us (97%)
  local copies, waits for them, and re-layouts  0.65 us (1%)
  between operations  0.65 us (1%)
    pallas_call x1, Pallas kernels, step(): pl.pallas_call(functools.partial(kernel, split, tiles), out_shape=[jax.Sh...  55.9 us

profile of v2, /device:TPU:6, one launch (start us, length us, event | category | flops | bytes accessed | tf_op | source)
XLA Modules:
  0.0 58.2 jit_solution(1221588911521109458)
XLA Ops:
  0.6 0.0 copy-start
  0.6 0.6 %copy-done = f32[16]{0:T(128)S(1)} copy-done((f32[16]{0:T(128)S(1)}, f32[16]{0:T(128)}, u32[]{:S(2)}) %copy-start) | copy-done | bytes 88
  1.3 55.9 %shard_map.119 = (f32[3,4,128,128]{3,2,1,0:T(8,128)S(1)}, f32[2,8,512]{2,1,0:T(8,128)S(1)}) custom-call(f32[128,512]{1,0:T(8,128)} %bitcast.8, f32[128,512]{1,0:T(8,128)} %bitcast.9, f32[128,512]{1,0:T(8,128)} %bitcast.10, bf16[2048,128]{1,0:T(8,128)(2,1)} %bitcast.7, f32[16]{0:T(128)S(1)} %copy-done, f32[8,512]{1,0:T(8,128)} %gas_rho_hbm.1, ...), custom_call_target="tpu_custom_call" | custom-call | tf_op jit(solution)/shard_map/pallas_call | solution.py:554
  57.2 1.0 %shard_map.120 = (f32[128,512]{1,0:T(8,128)}, f32[128,512]{1,0:T(8,128)}, f32[128,512]{1,0:T(8,128)}, f32[8,512]{1,0:T(8,128)}, f32[8,512]{1,0:T(8,128)}) custom-call(f32[3,4,128,128]{3,2,1,0:T(8,128)S(1)} %get-tuple-element.12.tiles, f32[2,8,512]{2,1,0:T(8,128)S(1)} %get-tuple-element.13.gas), custom_call_target="tpu_custom_call" | custom-call | tf_op jit(solution)/shard_map/pallas_call | solution.py:603
Async XLA Ops:
  0.6 0.7 %copy-start = (f32[16]{0:T(128)S(1)}, f32[16]{0:T(128)}, u32[]{:S(2)}) copy-start(f32[16]{0:T(128)} %stop.1) | copy-start | bytes 196

commit v3 on v2

--- a/solution.py
+++ b/solution.py
@@ -13,7 +13,7 @@
 QUAD = 4
 ROWS = 8
 LANES = 128
-CHUNKS = 2
+CHUNKS = 4
 DEEP = ROWS // CHUNKS
 VMEM_BYTES = 40 * 2**20
 ROW_ORDER = (2, 3, 4, 5, 0, 1, 6, 7)
@@ -56,7 +56,7 @@
     vr_hbm,
     va_hbm,
     coef_hbm,
-    stop,
+    stop_hbm,
     gas_rho_hbm,
     gas_vr_hbm,
     gas_va_hbm,
@@ -64,6 +64,7 @@
     gas_out,
     tiles_in,
     gas_in,
+    stop,
     own_coef,
     mate_coef,
     q_rows,
@@ -85,6 +86,7 @@
     halo_recv,
     give_send,
     item_recv,
+    own_send,
     up_send,
     down_send,
     gain_send_sem,
@@ -131,6 +133,8 @@
         pltpu.make_async_copy(src, gas_in.at[i], load_sem.at[3, 1 + i])
         for i, src in enumerate((gas_rho_hbm, gas_vr_hbm, gas_va_hbm))
     ]
+    load_stop = pltpu.make_async_copy(stop_hbm, stop, load_sem.at[4, 0])
+    load_stop.start()
     for group in loads:
         for load in group:
             load.start()
@@ -151,6 +155,7 @@
     prev_dev = (jnp.maximum(t - 1, 0), z)
     next_dev = (jnp.minimum(t + 1, tiles - 1), z)
 
+    load_stop.wait()
     stop_bin = lax.broadcasted_iota(jnp.int32, (bins, 1), 0)
     stop_col = jnp.zeros((bins, 1), F32)
     for b in range(bins):
@@ -291,8 +296,29 @@
                 def _():
                     pass_on(c, base + place, place, False).start()
 
-    def own_relay(c, far):
-        relay(c, far, own_base)
+    def own_items(c):
+        return [
+            pltpu.make_async_remote_copy(
+                src_ref=all_bins.at[c, z],
+                dst_ref=all_bins.at[c, z],
+                send_sem=own_send.at[c, i],
+                recv_sem=item_recv.at[c, z],
+                device_id=(t, quad_at(i)),
+                device_id_type=MESH,
+            )
+            for i in range(1, QUAD)
+        ]
+
+    def own_receive(c):
+        for i in range(1, QUAD):
+            pltpu.make_async_remote_copy(
+                src_ref=all_bins.at[c, quad_at(i)],
+                dst_ref=all_bins.at[c, quad_at(i)],
+                send_sem=own_send.at[c, i],
+                recv_sem=item_recv.at[c, quad_at(i)],
+                device_id=(t, quad_at(i)),
+                device_id_type=MESH,
+            ).wait_recv()
 
     def mate_relay(c, far):
         relay(c, far, other_base)
@@ -332,7 +358,8 @@
     def launch(c):
         all_bins[c, z] = halves[c, quad]
         give(c).start()
-        send_both(c, z)
+        for copy in own_items(c):
+            copy.start()
 
     def gains(c, coef, j):
         low = all_bins[c, :, j].reshape(2 * QUAD * bins, half)
@@ -463,39 +490,53 @@
     coef_from_mate.start()
     advect(0)
     launch(0)
+    advect(1)
+    launch(1)
     coef_from_mate.wait_recv()
     start(coef_y)
-    own_relay(0, 1)
     halo_in()
-    advect(1)
-    launch(1)
+    advect(2)
+    launch(2)
+    advect(3)
+    launch(3)
     start(spread)
     take_mates(0)
-    own_relay(0, 2)
     receive(coef_y)
     start(coef_x)
-    own_relay(1, 1)
+    take_mates(1)
     mate_relay(0, 1)
     sum_across()
-    own_relay(1, 2)
-    take_mates(1)
+    mate_relay(1, 1)
+    take_mates(2)
     mate_relay(0, 2)
+    take_mates(3)
+    mate_relay(1, 2)
+    mate_relay(2, 1)
     receive(coef_x)
     start(coef_core)
-    mate_relay(1, 1)
+    mate_relay(3, 1)
     gas_step()
     load_coef.wait()
-    own_relay(0, 3)
+    own_receive(0)
     mate_relay(0, 3)
-    mate_relay(1, 2)
+    mate_relay(2, 2)
     own_gains(0)
+    mate_relay(3, 2)
     receive(coef_core)
     mate_gains(0)
-    own_relay(1, 3)
+    own_receive(1)
     mate_relay(1, 3)
     mate_gains(1)
+    own_receive(2)
+    mate_relay(2, 3)
+    mate_gains(2)
+    own_receive(3)
+    mate_relay(3, 3)
+    mate_gains(3)
+    own_gains(1)
+    own_gains(2)
     dust_speeds()
-    own_gains(1)
+    own_gains(3)
     for c in range(CHUNKS):
         finish(c)
 
@@ -511,6 +552,8 @@
         copy.wait_send()
     for c in range(CHUNKS):
         give(c).wait_send()
+        for copy in own_items(c):
+            copy.wait_send()
         gain_copy(c).wait_send()
     for place in range(QUAD):
         for up in (True, False):
@@ -518,8 +561,8 @@
             @pl.when((can_up if up else can_down) & (place <= w if up else place >= w))
             def _():
                 pltpu.make_async_remote_copy(
-                    src_ref=all_bins.at[:, pl.ds(0, 2)],
-                    dst_ref=all_bins.at[:, pl.ds(0, 2)],
+                    src_ref=all_bins.at[:, pl.ds(0, 1)],
+                    dst_ref=all_bins.at[:, pl.ds(0, 1)],
                     send_sem=(up_send if up else down_send).at[place],
                     recv_sem=item_recv.at[0, 0],
                     device_id=(t, mate),
@@ -557,11 +600,12 @@
             jax.ShapeDtypeStruct((3, lane_tiles, flat[0], LANES), F32),
             jax.ShapeDtypeStruct((2, rows, cells), F32),
         ],
-        in_specs=[hbm] * 4 + [pl.BlockSpec(memory_space=pltpu.SMEM)] + [hbm] * 3,
+        in_specs=[hbm] * 8,
         out_specs=[vmem] * 2,
         scratch_shapes=[
             pltpu.VMEM((3, lane_tiles, flat[0], LANES), F32),
             pltpu.VMEM((3, rows, cells), F32),
+            pltpu.SMEM((bins,), F32),
             pltpu.VMEM(coef.shape, BF16),
             pltpu.VMEM((cores, xs, ys, coef.shape[0] // (cores * xs * ys), total_bins), BF16),
             pltpu.VMEM((rows + 4, bins, cells), F32),
@@ -578,11 +622,12 @@
             pltpu.VMEM((QUAD, 4, cells), F32),
             pltpu.VMEM((CHUNKS, DEEP, bins, half), BF16),
             pltpu.VMEM((CHUNKS, DEEP, bins, half), BF16),
-            dma((4, lane_tiles)),
+            dma((5, lane_tiles)),
             dma((2,)),
             dma((2,)),
             dma((CHUNKS,)),
             dma((CHUNKS, 2 * QUAD)),
+            dma((CHUNKS, QUAD)),
             dma((QUAD,)),
             dma((QUAD,)),
             dma((CHUNKS,)),
@@ -596,9 +641,10 @@
             collective_id=0, has_side_effects=True, vmem_limit_bytes=VMEM_BYTES
         ),
     )(
-        *(pltpu.with_memory_space_constraint(x, pltpu.HBM) for x in (rho.reshape(flat), vr.reshape(flat), va.reshape(flat), coef)),
-        stop,
-        *(pltpu.with_memory_space_constraint(x, pltpu.HBM) for x in (gas_rho, gas_vr, gas_va)),
+        *(
+            pltpu.with_memory_space_constraint(x, pltpu.HBM)
+            for x in (rho.reshape(flat), vr.reshape(flat), va.reshape(flat), coef, stop, gas_rho, gas_vr, gas_va)
+        )
     )
     outs = pl.pallas_call(
         write_out,

time: 58.4 us -> 57.2 us (0.979)
  local copies, waits for them, and re-layouts: 0.65 us -> 0 us
    unnamed x2 -> x0, local copies, waits for them, and re-layouts: 0.65 us -> none
where the time goes in v3:
time: 57.2 us; the launch traced here: 57.1 us
  Pallas kernels  56.4 us (99%)
  between operations  0.64 us (1%)
    pallas_call x1, Pallas kernels, step(): pl.pallas_call(functools.partial(kernel, split, tiles), out_shape=[jax.Sh...  55.4 us

profile of v3, /device:TPU:6, one launch (start us, length us, event | category | flops | bytes accessed | tf_op | source)
XLA Modules:
  0.0 57.1 jit_solution(12964265816031050603)
XLA Ops:
  0.6 55.4 %shard_map.119 = (f32[3,4,128,128]{3,2,1,0:T(8,128)S(1)}, f32[2,8,512]{2,1,0:T(8,128)S(1)}) custom-call(f32[128,512]{1,0:T(8,128)} %bitcast.8, f32[128,512]{1,0:T(8,128)} %bitcast.9, f32[128,512]{1,0:T(8,128)} %bitcast.10, bf16[2048,128]{1,0:T(8,128)(2,1)} %bitcast.7, f32[16]{0:T(128)} %stop_hbm.1, f32[8,512]{1,0:T(8,128)} %gas_rho_hbm.1, ...), custom_call_target="tpu_custom_call" | custom-call | tf_op jit(solution)/shard_map/pallas_call | solution.py:597
  56.1 1.0 %shard_map.120 = (f32[128,512]{1,0:T(8,128)}, f32[128,512]{1,0:T(8,128)}, f32[128,512]{1,0:T(8,128)}, f32[8,512]{1,0:T(8,128)}, f32[8,512]{1,0:T(8,128)}) custom-call(f32[3,4,128,128]{3,2,1,0:T(8,128)S(1)} %get-tuple-element.12.tiles, f32[2,8,512]{2,1,0:T(8,128)S(1)} %get-tuple-element.13.gas), custom_call_target="tpu_custom_call" | custom-call | tf_op jit(solution)/shard_map/pallas_call | solution.py:649

commit v4 on v3

--- a/solution.py
+++ b/solution.py
@@ -164,12 +164,15 @@
     keep = stop_col * couple
 
     partial[...] = jnp.zeros_like(partial)
-    for group, rows, first in zip(loads, (q_rows, v_rows, a_rows), (2, 1, 0)):
-        i = 2 - first
-        for l, load in enumerate(group):
+
+    def unpack(i, rows, first):
+        for l, load in enumerate(loads[i]):
             load.wait()
             for r in range(ROWS):
                 rows[first + r, :, lane_tile(l)] = tiles_in[i, l, pl.ds(r, bins, stride=ROWS), :]
+
+    unpack(0, q_rows, 2)
+    unpack(1, v_rows, 1)
 
     def put(i, r, value):
         for l in range(lane_tiles):
@@ -488,6 +491,7 @@
             copy.wait_recv()
 
     coef_from_mate.start()
+    unpack(2, a_rows, 0)
     advect(0)
     launch(0)
     advect(1)

time: 57.2 us -> 56.7 us (level)
    pallas_call x1, Pallas kernels: 55.4 us -> 54.9 us  [step(): pl.pallas_call(functools.partial(kernel, split, tiles), out_shape=[jax.Sh...]
where the time goes in v4:
time: 56.7 us; the launch traced here: 56.5 us
  Pallas kernels  55.9 us (99%)
  between operations  0.64 us (1%)
    pallas_call x1, Pallas kernels, step(): pl.pallas_call(functools.partial(kernel, split, tiles), out_shape=[jax.Sh...  54.9 us

profile of v4, /device:TPU:6, one launch (start us, length us, event | category | flops | bytes accessed | tf_op | source)
XLA Modules:
  0.0 56.5 jit_solution(12248793584027607251)
XLA Ops:
  0.6 54.9 %shard_map.119 = (f32[3,4,128,128]{3,2,1,0:T(8,128)S(1)}, f32[2,8,512]{2,1,0:T(8,128)S(1)}) custom-call(f32[128,512]{1,0:T(8,128)} %bitcast.8, f32[128,512]{1,0:T(8,128)} %bitcast.9, f32[128,512]{1,0:T(8,128)} %bitcast.10, bf16[2048,128]{1,0:T(8,128)(2,1)} %bitcast.7, f32[16]{0:T(128)} %stop_hbm.1, f32[8,512]{1,0:T(8,128)} %gas_rho_hbm.1, ...), custom_call_target="tpu_custom_call" | custom-call | tf_op jit(solution)/shard_map/pallas_call | solution.py:601
  55.5 1.0 %shard_map.120 = (f32[128,512]{1,0:T(8,128)}, f32[128,512]{1,0:T(8,128)}, f32[128,512]{1,0:T(8,128)}, f32[8,512]{1,0:T(8,128)}, f32[8,512]{1,0:T(8,128)}) custom-call(f32[3,4,128,128]{3,2,1,0:T(8,128)S(1)} %get-tuple-element.12.tiles, f32[2,8,512]{2,1,0:T(8,128)S(1)} %get-tuple-element.13.gas), custom_call_target="tpu_custom_call" | custom-call | tf_op jit(solution)/shard_map/pallas_call | solution.py:653
